TPU v7x, 32 devices: a whole 2x2x4 slice. The times are simulated.
32 devices in a mesh: dp: 8 (over y, x, core), neg: 4 (over z).
Axes of the slice: x: 2, y: 2, z: 4, core: 2. Of those that a mesh axis runs over, the one named last changes fastest.
Arguments:
- img_features: bfloat16 [64, 256, 1024], P(('dp', 'neg'))
- txt_features: bfloat16 [64, 64, 1024], P(('dp', 'neg'))
- w_img: bfloat16 [1024, 256], replicated
- w_txt: bfloat16 [1024, 256], replicated
- cap_len: int32 [64], P(('dp', 'neg')), may hold values from 16 to 64
- pairs: int32 [8, 8], P('dp'), may hold values from 0 to 7, each once within a row
Outputs:
- grad_img_features: bfloat16 [64, 256, 1024], P(('dp', 'neg'))
- grad_txt_features: bfloat16 [64, 64, 1024], P(('dp', 'neg'))
- grad_w_img: float32 [1024, 256], P('dp')
- grad_w_txt: float32 [1024, 256], P('dp')
Inputs may be any that keep to these rules, and one draw needn't show every extreme that they name: `pairs`: each row is a permutation of 0 to 7.
All inputs are finite; a program needn't handle non-finite values.
Results may differ from a plain program's by a relative error of at most 0.011.
Values may be sent and summed in bfloat16 or wider, within the bound.
A program may use at most 64 MiB of HBM per device.

v0:
```python
import jax
import jax.numpy as jnp
from jax import lax
from jax.sharding import PartitionSpec as P

TOKEN_SCALE = 100.0
PAIR_SCALE = 50.0
EPSILON = 1e-06


def combined_all(value, axis, join):
    pieces = jax.tree.map(lambda part: lax.all_gather(part, axis), value)
    head = jax.tree.map(lambda part: part[0], pieces)
    tail = jax.tree.map(lambda part: part[1:], pieces)
    subtotal, _ = lax.scan(lambda subtotal, share: (join(subtotal, share), None), head, tail)
    return subtotal


def unit_rows(projected):
    inverse = lax.rsqrt(jnp.sum(projected * projected, axis=-1, keepdims=True) + EPSILON)
    return (projected * inverse, inverse)


def back_unit(gradient, unit, inverse):
    return (gradient - unit * jnp.sum(unit * gradient, axis=-1, keepdims=True)) * inverse


def token_pool(scores, lengths, count_caps, text_len):
    rows = scores.shape[0]
    logits = (TOKEN_SCALE * scores).reshape(rows, count_caps, text_len)
    valid = (jnp.arange(text_len, dtype=jnp.int32)[None, :] < lengths[:, None])[None]
    peaks = jnp.max(jnp.where(valid, logits, -jnp.inf), axis=2, keepdims=True)
    expos = jnp.where(valid, jnp.exp(logits - peaks), 0.0)
    totals = jnp.sum(expos, axis=2, keepdims=True)
    pooled = (peaks[..., 0] + jnp.log(totals[..., 0])) / TOKEN_SCALE
    return (pooled, expos / totals)


def merge_stats(first, second):
    top = jnp.maximum(first[0], second[0])
    return (top, first[1] * jnp.exp(first[0] - top) + second[1] * jnp.exp(second[0] - top))


def shards(img_features, txt_features, w_img, w_txt, cap_len, pairs):
    local_count = img_features.shape[0]
    img_len = img_features.shape[1]
    text_len = txt_features.shape[1]
    width = w_img.shape[1]
    img_flat = img_features.reshape(local_count * img_len, img_features.shape[2])
    txt_flat = txt_features.reshape(local_count * text_len, txt_features.shape[2])
    img_unit, img_inv = unit_rows(jnp.dot(img_flat, w_img, preferred_element_type=jnp.float32))
    txt_unit, txt_inv = unit_rows(jnp.dot(txt_flat, w_txt, preferred_element_type=jnp.float32))
    img_half = img_unit.astype(jnp.bfloat16)
    txt_half = txt_unit.astype(jnp.bfloat16)
    group_text, group_len = (
        lax.all_gather(txt_half.reshape(local_count, text_len, width), "neg", axis=0, tiled=True),
        lax.all_gather(cap_len, "neg", axis=0, tiled=True),
    )
    group_size = group_text.shape[0]
    text_rows = group_text.reshape(group_size * text_len, width)
    scores = jnp.dot(img_half, text_rows.T, preferred_element_type=jnp.float32)
    pooled, weights = token_pool(scores, group_len, group_size, text_len)
    logits = PAIR_SCALE * jnp.mean(pooled.reshape(local_count, img_len, group_size), axis=1)
    row_prob = jax.nn.softmax(logits, axis=1)
    local_top = jnp.max(logits, axis=0)
    local_sum = jnp.sum(jnp.exp(logits - local_top[None, :]), axis=0)
    col_top, col_sum = combined_all((local_top, local_sum), "neg", merge_stats)
    col_prob = jnp.exp(logits - col_top[None, :]) / col_sum[None, :]
    start = lax.axis_index("neg") * local_count
    perm = lax.dynamic_slice_in_dim(pairs[0], start, local_count)
    target = (perm[:, None] == jnp.arange(group_size, dtype=jnp.int32)[None, :]).astype(jnp.float32)
    pair_grad = (row_prob + col_prob - 2.0 * target) * (PAIR_SCALE / (2.0 * group_size * img_len))
    spread = jnp.broadcast_to(pair_grad[:, None, :], (local_count, img_len, group_size))
    spread = spread.reshape(local_count * img_len, group_size, 1)
    score_grad = (
        (spread * weights)
        .reshape(local_count * img_len, group_size * text_len)
        .astype(jnp.bfloat16)
    )
    img_grad = jnp.dot(score_grad, text_rows, preferred_element_type=jnp.float32)
    text_terms = jnp.dot(score_grad.T, img_half, preferred_element_type=jnp.float32)
    txt_grad = lax.psum_scatter(
        text_terms.reshape(group_size, text_len, width), "neg", scatter_dimension=0, tiled=True
    )
    txt_grad = txt_grad.reshape(local_count * text_len, width)
    img_back = back_unit(img_grad, img_unit, img_inv).astype(jnp.bfloat16)
    txt_back = back_unit(txt_grad, txt_unit, txt_inv).astype(jnp.bfloat16)
    feat_img = jnp.dot(img_back, w_img.T, preferred_element_type=jnp.float32).astype(jnp.bfloat16)
    feat_txt = jnp.dot(txt_back, w_txt.T, preferred_element_type=jnp.float32).astype(jnp.bfloat16)
    wgrad_img = jnp.dot(img_flat.T, img_back, preferred_element_type=jnp.float32)
    wgrad_txt = jnp.dot(txt_flat.T, txt_back, preferred_element_type=jnp.float32)
    summed_img, summed_txt = lax.psum((wgrad_img, wgrad_txt), "neg")
    final_img, final_txt = (
        lax.psum_scatter(summed_img, "dp", scatter_dimension=0, tiled=True),
        lax.psum_scatter(summed_txt, "dp", scatter_dimension=0, tiled=True),
    )
    return (
        feat_img.reshape(img_features.shape),
        feat_txt.reshape(txt_features.shape),
        final_img,
        final_txt,
    )


def solution(mesh):
    in_specs = (
        P(("dp", "neg"), None, None),
        P(("dp", "neg"), None, None),
        P(),
        P(),
        P(("dp", "neg")),
        P("dp", None),
    )
    out_specs = (
        P(("dp", "neg"), None, None),
        P(("dp", "neg"), None, None),
        P("dp", None),
        P("dp", None),
    )
    return jax.shard_map(shards, mesh=mesh, in_specs=in_specs, out_specs=out_specs, check_vma=False)
```

profile of v0, /device:TPU:0, one launch (start us, length us, event | category | flops | bytes accessed | tf_op | source)
XLA Modules:
  0.0 198.3 jit_solution(17703134065942957561)
XLA Ops:
  7.2 0.0 copy-start
  7.2 0.0 copy-start.1
  7.2 0.0 reduce-scatter.4.cloned.1.call-start
  7.2 1.3 dynamic-slice.1
  9.3 0.9 dynamic-update-slice
  10.1 9.9 %all-reduce = s32[8]{0:T(128)S(1)} all-reduce(s32[8]{0:T(128)S(1)} %dynamic-update-slice), channel_id=1, replica_groups=mesh['dp'=8,'neg'=4] {'neg'}, use_global_device_ids=true, to_apply=%add | all-reduce | flops 8 | bytes 64
  20.0 0.1 iota_compare_fusion
  20.1 0.1 broadcast_reduce_fusion
  20.8 0.1 lt.41
  20.9 0.1 lt.39
  21.0 1.4 multiply_reduce_fusion.2
  22.4 0.0 copy-start.8
  22.4 0.1 multiply_convert_fusion.2
  22.5 13.8 %all_gather.19 = bf16[8,64,256]{2,1,0:T(8,128)(2,1)S(1)} all-gather(bf16[2,64,256]{2,1,0:T(8,128)(2,1)S(1)} %bitcast.91), channel_id=1, replica_groups=mesh['dp'=8,'neg'=4] {'neg'}, dimensions={0}, use_global_device_ids=true | all-gather | bytes 327680 | tf_op jit(solution)/shard_map/all_gather | solution.py:56
  36.3 0.0 copy-done
  36.3 0.5 multiply_reduce_fusion.1
  36.8 0.0 copy-start.6
  36.9 0.3 select_reduce_fusion.1
  37.2 0.0 copy-start.10
  37.2 0.2 copy-done.6
  37.4 0.3 select_reduce_fusion
  37.7 0.0 copy-start.5
  37.7 0.6 copy-done.5
  38.3 0.1 reduce_sum.75
  38.4 0.1 fusion.18
  38.5 0.2 fusion.15
  38.8 0.2 dynamic-update-slice.1
  39.0 0.2 dynamic-update-slice.2
  39.2 10.6 %all-reduce.3 = (f32[32]{0:T(128)S(1)}, f32[32]{0:T(128)S(1)}) all-reduce(f32[32]{0:T(128)S(1)} %dynamic-update-slice.1, f32[32]{0:T(128)S(1)} %dynamic-update-slice.2), channel_id=2, replica_groups=mesh['dp'=8,'neg'=4] {'neg'}, use_global_device_ids=true, to_apply=%add.1 | all-reduce | flops 64 | bytes 512
  49.8 0.1 slice.18
  49.9 0.1 slice.19
  50.0 0.1 reshape.181
  50.1 0.1 reshape.180
  50.1 0.1 while.12
  50.3 0.0 copy-done.10
  50.3 0.1 dynamic-slice_bitcast_fusion
  50.3 0.1 fusion.16
  50.4 0.1 broadcast_in_dim.27
  50.5 1.0 fusion.6
  51.5 0.0 copy-start.7
  51.5 1.9 fusion.9
  53.4 0.0 reduce-scatter.4.cloned.1.call-update
  53.4 0.0 reduce-scatter.6.cloned.1.call-start
  53.5 0.4 multiply_reduce_fusion
  53.8 0.1 multiply_convert_fusion
  53.9 1.4 convolution_bitcast_fusion.1
  55.4 0.0 reduce-scatter.6.cloned.1.call-update
  55.4 0.0 reduce-scatter.8.cloned.1.call-start
  55.4 17.9 %reduce-scatter.4.cloned.1.call-done = f32[2,64,256]{2,1,0:T(8,128)} async-done(((f32[8,64,256]{2,1,0:T(8,128)}), f32[2,64,256]{2,1,0:T(8,128)}) %reduce-scatter.4.cloned.1.call-update) | async-done | bytes 131088 | tf_op jit(solution)/shard_map/reduce_scatter | solution.py:82
  73.4 0.0 copy-done.9
  73.4 1.1 fusion.11
  74.5 1.0 fusion.13
  75.5 0.0 copy-start.2
  75.5 1.3 convolution_bitcast_fusion
  76.8 0.0 reduce-scatter.8.cloned.1.call-update
  76.8 0.0 all-reduce.7.cloned.1.call-start
  76.9 34.5 %reduce-scatter.6.cloned.1.call-done = f32[128,256]{0,1:T(8,128)} async-done(((f32[1024,256]{0,1:T(8,128)}), f32[128,256]{0,1:T(8,128)}) %reduce-scatter.6.cloned.1.call-update) | async-done | bytes 131088 | tf_op jit(solution)/shard_map/reduce_scatter | solution.py:94
  111.4 39.2 %reduce-scatter.8.cloned.1.call-done = f32[128,256]{0,1:T(8,128)} async-done(((f32[1024,256]{0,1:T(8,128)}), f32[128,256]{0,1:T(8,128)}) %reduce-scatter.8.cloned.1.call-update) | async-done | bytes 131088 | tf_op jit(solution)/shard_map/reduce_scatter | solution.py:95
  150.7 0.0 all-reduce.7.cloned.1.call-update
  150.7 1.5 convolution_convert_fusion
  152.2 1.0 convolution_convert_fusion.1
  153.2 35.3 %all-reduce.7.cloned.1.call-done = (f32[128,256]{0,1:T(8,128)}, f32[128,256]{0,1:T(8,128)}) async-done(((f32[128,256]{0,1:T(8,128)}, f32[128,256]{0,1:T(8,128)}), (f32[128,256]{0,1:T(8,128)}, f32[128,256]{0,1:T(8,128)})) %all-reduce.7.cloned.1.call-update) | async-done | bytes 262160 | tf_op jit(solution)/shard_map/psum | solution.py:92
  188.4 1.7 copy.14
  190.1 1.7 copy.15
  (21 shorter events, 0.2 us)
Async XLA Ops:
  7.2 29.2 %copy-start = (bf16[2,256,1024]{2,1,0:T(8,128)(2,1)S(1)}, bf16[2,256,1024]{2,1,0:T(8,128)(2,1)}, u32[]{:S(2)}) copy-start(bf16[2,256,1024]{2,1,0:T(8,128)(2,1)} %param.8) | copy-start | bytes 3145732
  7.2 29.1 %copy-start.1 = (bf16[1024,256]{1,0:T(8,128)(2,1)S(1)}, bf16[1024,256]{1,0:T(8,128)(2,1)}, u32[]{:S(2)}) copy-start(bf16[1024,256]{1,0:T(8,128)(2,1)} %param.10) | copy-start | bytes 1572868
  7.2 66.2 %reduce-scatter.4.cloned.1.call-start = ((), (), s32[]{:S(2)}) async-start(), calls=%async_computation.3 | async-start | bytes 655360 | tf_op jit(solution)/shard_map/reduce_scatter | solution.py:82
  22.4 14.4 %copy-start.8 = (f32[128]{0:T(128)}, f32[128]{0:T(128)S(1)}, u32[]{:S(2)}) copy-start(f32[128]{0:T(128)S(1)} %add_rsqrt_fusion.1) | copy-start | bytes 1540
  36.8 0.6 copy-start.6
  37.2 13.1 %copy-start.10 = (s32[1,8]{1,0:T(1,128)S(1)}, s32[1,8]{1,0:T(1,128)}, u32[]{:S(2)}) copy-start(s32[1,8]{1,0:T(1,128)} %param.13) | copy-start | bytes 100
  37.7 0.6 copy-start.5
  51.5 2.0 copy-start.7
  53.4 58.0 %reduce-scatter.6.cloned.1.call-start = ((), (), s32[]{:S(2)}) async-start(), calls=%async_computation.4 | async-start | bytes 1179648 | tf_op jit(solution)/shard_map/reduce_scatter | solution.py:94
  55.4 18.0 %copy-start.9 = (f32[128]{0:T(128)S(1)}, f32[128]{0:T(128)}, u32[]{:S(2)}) copy-start(f32[128]{0:T(128)} %copy-done.8) | copy-start | bytes 1540
  55.4 20.1 %copy-start.4 = (bf16[2,64,1024]{2,1,0:T(8,128)(2,1)S(1)}, bf16[2,64,1024]{2,1,0:T(8,128)(2,1)}, u32[]{:S(2)}) copy-start(bf16[2,64,1024]{2,1,0:T(8,128)(2,1)} %param.9) | copy-start | bytes 786436
  55.4 95.3 %reduce-scatter.8.cloned.1.call-start = ((), (), s32[]{:S(2)}) async-start(), calls=%async_computation.5 | async-start | bytes 1179648 | tf_op jit(solution)/shard_map/reduce_scatter | solution.py:95
  75.5 75.2 %copy-start.2 = (bf16[1024,256]{1,0:T(8,128)(2,1)S(1)}, bf16[1024,256]{1,0:T(8,128)(2,1)}, u32[]{:S(2)}) copy-start(bf16[1024,256]{1,0:T(8,128)(2,1)} %param.10) | copy-start | bytes 1572868
  76.8 111.6 %all-reduce.7.cloned.1.call-start = ((), (), s32[]{:S(2)}) async-start(), calls=%async_computation.6 | async-start | bytes 524288 | tf_op jit(solution)/shard_map/psum | solution.py:92
  150.7 1.5 copy-start.3
Sparse Core Ops, SparseCore 0:
  53.5 19.8 reduce-scatter.3
  77.1 34.2 reduce-scatter.5
  114.6 36.0 reduce-scatter.7
  152.9 35.5 all-reduce.6
where the time goes:
time: 199 us; the launch traced here: 198 us
  waiting for transfers between devices  127 us (64%)
  blocking collectives  34.3 us (17%)
  between operations  15.3 us (8%)
  matrix products  9.68 us (5%)
  local copies, waits for them, and re-layouts  7.56 us (4%)
  other arithmetic  4.22 us (2%)
    reduce_scatter x1, waiting for transfers between devices, shards(): lax.psum_scatter(summed_txt, 'dp', scatter_dimension=0, tiled=True)  39.2 us
    psum x1, waiting for transfers between devices, shards(): summed_img, summed_txt = lax.psum((wgrad_img, wgrad_txt), 'neg')  35.3 us
    reduce_scatter x1, waiting for transfers between devices, shards(): lax.psum_scatter(summed_img, 'dp', scatter_dimension=0, tiled=True)  34.5 us
    unnamed x2, blocking collectives  20.5 us
    reduce_scatter x1, waiting for transfers between devices, shards(): lax.psum_scatter(text_terms.reshape(group_size, text_len, width), 'neg',...  17.9 us
    all_gather x1, blocking collectives, shards(): lax.all_gather(txt_half.reshape(local_count, text_len, width), 'neg', axi...  13.8 us
    unnamed x31, local copies, waits for them, and re-layouts  6.85 us
  transfers between devices with their start and end apart: 4, of which 4 were waited for; matrix products, arithmetic and copies ran while one was open for 4% of the time, Pallas kernels for 0%

commit v1 on v0

v1 whole, which is shorter than its diff:
```python
import functools

import jax
import jax.numpy as jnp
from jax import lax
from jax.experimental import pallas as pl
from jax.experimental.pallas import tpu as pltpu
from jax.sharding import PartitionSpec as P

TOKEN_SCALE = 100.0
PAIR_SCALE = 50.0
EPSILON = 1e-06
MARK = 4.0
LOW = -1e30
BF = jnp.bfloat16
F32 = jnp.float32
MESH = pl.DeviceIdType.MESH


def nn(a, b):
    return lax.dot_general(a, b, (((1,), (0,)), ((), ())), preferred_element_type=F32)


def nt(a, b):
    return lax.dot_general(a, b, (((1,), (1,)), ((), ())), preferred_element_type=F32)


def unit_rows(projected):
    inverse = lax.rsqrt(jnp.sum(projected * projected, axis=-1, keepdims=True) + EPSILON)
    return projected * inverse, inverse


def back_unit(gradient, unit, inverse):
    return (gradient - unit * jnp.sum(unit * gradient, axis=-1, keepdims=True)) * inverse


class Exchange:
    def __init__(self, me, n, device, slots, send, recv):
        self.me, self.n, self.device = me, n, device
        self.slots, self.send, self.recv = slots, send, recv
        self.started = []

    def peer(self, offset):
        return lax.rem(self.me + offset, self.n)

    def start(self, offset, source):
        copy = pltpu.make_async_remote_copy(
            src_ref=source,
            dst_ref=self.slots.at[self.me],
            send_sem=self.send.at[offset],
            recv_sem=self.recv.at[self.me],
            device_id=self.device(self.peer(offset)),
            device_id_type=MESH,
        )
        copy.start()
        self.started.append(copy)

    def take(self, offset):
        other = self.peer(offset)
        pltpu.make_async_remote_copy(
            src_ref=self.slots.at[other],
            dst_ref=self.slots.at[other],
            send_sem=self.send.at[offset],
            recv_sem=self.recv.at[other],
            device_id=self.device(other),
            device_id_type=MESH,
        ).wait_recv()
        return other

    def finish(self):
        for copy in self.started:
            copy.wait_send()


def kernel(
    dims,
    img_hbm, txt_hbm, wi_hbm, wt_hbm, cap, pairs,
    fi_hbm, ft_hbm, gi_out, gt_out,
    img, txt, wi, wt, img_t, txt_t,
    img_unit, img_inv, img_half, txt_unit, txt_inv,
    text_all, expo, total, logit_all, sg, terms, own_term, term_in,
    img_back, txt_back, wg, core_out, core_in, plane_out, plane_own, plane_in,
    part, part_out, ring_in, full, fi, ft,
    load_sem, save_sem,
    text_s, text_r, logit_s, logit_r, term_s, term_r,
    core_s, core_r, plane_s, plane_r, ring_s, ring_r, full_s, full_r,
):
    L, PI, T, D, W, N, NDP = dims
    H = NDP // 2
    r = D // NDP
    rows_i, rows_t = L * PI, L * T
    dp = lax.axis_index("dp")
    me = lax.axis_index("neg")
    core = lax.rem(dp, 2)
    chip = lax.div(dp, 2)
    split = r % (16 * N) == 0
    rr = r // N if split else r

    loads = [
        pltpu.make_async_copy(source, target, load_sem.at[i])
        for i, (source, target) in enumerate(
            ((txt_hbm, txt), (wt_hbm, wt), (wi_hbm, wi), (img_hbm, img))
        )
    ]
    for load in loads:
        load.start()

    def on_neg(k):
        return (dp, k)

    def on_plane(k):
        return (k * 2 + core, me)

    barrier = pltpu.get_barrier_semaphore()
    for o in range(1, N):
        pl.semaphore_signal(barrier, inc=1, device_id=on_neg(lax.rem(me + o, N)), device_id_type=MESH)
    for o in range(1, H):
        pl.semaphore_signal(
            barrier, inc=1, device_id=on_plane(lax.rem(chip + o, H)), device_id_type=MESH
        )
    mate = (chip * 2 + 1 - core, me)
    pl.semaphore_signal(barrier, inc=1, device_id=mate, device_id_type=MESH)

    loads[0].wait()
    loads[1].wait()
    unit, inverse = unit_rows(nn(txt[...], wt[...]))
    txt_unit[...] = unit
    txt_inv[...] = inverse
    place = lax.broadcasted_iota(jnp.int32, (T, W), 0)
    for c in range(L):
        text_all[me, c * T:(c + 1) * T, :] = jnp.where(
            place < cap[c], unit[c * T:(c + 1) * T], MARK
        ).astype(BF)
    pl.semaphore_wait(barrier, N - 1 + H - 1 + 1)
    text_x = Exchange(me, N, on_neg, text_all, text_s, text_r)
    for o in range(1, N):
        text_x.start(o, text_all.at[me])

    loads[2].wait()
    loads[3].wait()
    for i in range(L):
        rows = slice(i * PI, (i + 1) * PI)
        unit, inverse = unit_rows(nn(img[rows, :], wi[...]))
        img_unit[rows, :] = unit
        img_inv[rows, :] = inverse
        img_half[rows, :] = unit.astype(BF)

    def transpose_features():
        for d in range(0, D, 256):
            for i in range(L):
                img_t[d:d + 256, i * PI:(i + 1) * PI] = img[i * PI:(i + 1) * PI, d:d + 256].T
            txt_t[d:d + 256, :] = txt[:, d:d + 256].T

    lane = lax.broadcasted_iota(jnp.int32, (8, 128), 1)
    line = lax.broadcasted_iota(jnp.int32, (8, 128), 0)

    def pool(j):
        text = text_all[j]
        marks = text[:, 0:128].astype(F32)
        marks = jnp.concatenate([marks] * (rows_i // 128), axis=1)
        scores = jnp.where(marks < 2.0, TOKEN_SCALE * nt(text, img_half[...]), LOW)
        scores = scores.reshape(L, T, rows_i)
        peaks = jnp.max(scores, axis=1, keepdims=True)
        expos = jnp.exp(scores - peaks)
        totals = jnp.sum(expos, axis=1)
        expo[j] = expos.reshape(rows_t, rows_i)
        total[j] = jnp.concatenate([totals, jnp.ones((8 - L, rows_i), F32)], axis=0)
        pooled = peaks[:, 0, :] + jnp.log(totals)
        pooled = jnp.concatenate([pooled, jnp.zeros((8 - L, rows_i), F32)], axis=0)
        tile = jnp.full((8, 128), LOW, F32)
        for i in range(L):
            mean = jnp.sum(pooled[:, i * PI:(i + 1) * PI], axis=1, keepdims=True)
            mean = mean * (PAIR_SCALE / (TOKEN_SCALE * PI))
            tile = jnp.where((lane == i) & (line < L), mean, tile)
        logit_all[me, j] = tile

    pool(me)
    transpose_features()
    for o in range(1, N):
        pool(text_x.take(o))
    logit_x = Exchange(me, N, on_neg, logit_all, logit_s, logit_r)
    for o in range(1, N):
        logit_x.start(o, logit_all.at[me])
    own = logit_all[me]
    row_top = jnp.max(jnp.max(own, axis=0), axis=0, keepdims=True)
    row_exp = jnp.exp(own - row_top[None])
    row_prob = row_exp / jnp.sum(jnp.sum(row_exp, axis=0), axis=0, keepdims=True)[None]
    caption = lax.broadcasted_iota(jnp.int32, (N, 8, 128), 0) * L + lax.broadcasted_iota(
        jnp.int32, (N, 8, 128), 1
    )
    lanes = lax.broadcasted_iota(jnp.int32, (N, 8, 128), 2)
    target = jnp.zeros((N, 8, 128), F32)
    for i in range(L):
        target = jnp.where((lanes == i) & (caption == pairs[0, me * L + i]), 1.0, target)
    for o in range(1, N):
        logit_x.take(o)
    everyone = logit_all[...]
    col_top = jnp.max(jnp.max(everyone, axis=0), axis=-1, keepdims=True)
    col_sum = jnp.sum(
        jnp.sum(jnp.exp(everyone - col_top[None]), axis=0), axis=-1, keepdims=True
    )
    col_prob = jnp.exp(own - col_top) / col_sum
    pair_grad = (row_prob + col_prob - 2.0 * target) * (PAIR_SCALE / (2.0 * N * L * PI))
    own_logits = logit_all.at[me]
    logit_x.finish()
    own_logits[...] = pair_grad

    term_x = Exchange(me, N, on_neg, term_in, term_s, term_r)
    for o in list(range(1, N)) + [0]:
        j = lax.rem(me + o, N)
        pair = own_logits[j]
        spread = jnp.concatenate(
            [jnp.broadcast_to(pair[:, i:i + 1], (8, PI)) for i in range(L)], axis=1
        )
        factor = spread / total[j]
        shares = []
        for c in range(L):
            shares.append((expo[j, c * T:(c + 1) * T, :] * factor[c:c + 1, :]).astype(BF))
        share = jnp.concatenate(shares, axis=0)
        sg[j] = share
        term = nn(share, img_half[...])
        if o == 0:
            own_term[...] = term
        else:
            terms[o] = term.astype(BF)
            term_x.start(o, terms.at[o])

    texts = text_all[...].reshape(N * rows_t, W)
    for i in range(L):
        rows = slice(i * PI, (i + 1) * PI)
        grad = nn(sg[:, :, rows].reshape(N * rows_t, PI).T, texts)
        img_back[rows, :] = back_unit(grad, img_unit[rows, :], img_inv[rows, :]).astype(BF)

    cores = []

    def core_copy(m):
        return pltpu.make_async_remote_copy(
            src_ref=core_out.at[m],
            dst_ref=core_in.at[m],
            send_sem=core_s.at[m],
            recv_sem=core_r.at[m],
            device_id=mate,
            device_id_type=MESH,
        )

    def weight_grad(m, features_t, back):
        step = max(256, r)
        for d in range(0, D, step):
            out = nn(features_t[d:d + step, :], back[...])
            for k in range(d // r, (d + step) // r):
                wg[m, k % 2, k // 2] = out[k * r - d:(k + 1) * r - d]
        core_out[m] = wg[m, 1 - core].astype(BF)
        copy = core_copy(m)
        copy.start()
        cores.append(copy)

    planes = [
        Exchange(chip, H, on_plane, plane_in.at[m], plane_s.at[m], plane_r.at[m]) for m in range(2)
    ]
    rings = [Exchange(me, N, on_neg, ring_in.at[m], ring_s.at[m], ring_r.at[m]) for m in range(2)]
    fulls = [Exchange(me, N, on_neg, full.at[m], full_s.at[m], full_r.at[m]) for m in range(2)]

    def plane_send(m):
        cores[m].wait_recv()
        for o in range(1, H):
            k = planes[m].peer(o)
            plane_out[m, o] = (wg[m, core, k] + core_in[m, k].astype(F32)).astype(BF)
            planes[m].start(o, plane_out.at[m, o])
        plane_own[m] = wg[m, core, chip] + core_in[m, chip].astype(F32)

    def ring_send(m):
        value = plane_own[m]
        for o in range(1, H):
            value = value + plane_in[m, planes[m].take(o)].astype(F32)
        if split:
            value = value.reshape(N, rr, W)
            part[m] = value
            part_out[m] = value.astype(BF)
            for o in range(1, N):
                rings[m].start(o, part_out.at[m, rings[m].peer(o)])
        else:
            ring_in[m, me] = value.astype(BF)
            for o in range(1, N):
                rings[m].start(o, ring_in.at[m, me])

    def full_send(m):
        if split:
            value = part[m, me]
            for o in range(1, N):
                value = value + ring_in[m, rings[m].take(o)].astype(F32)
            full[m, me] = value.astype(BF)
            for o in range(1, N):
                fulls[m].start(o, full.at[m, me])

    def result(m, out):
        if split:
            for o in range(1, N):
                fulls[m].take(o)
            out[...] = full[m].astype(F32).reshape(r, W)
        else:
            for o in range(1, N):
                rings[m].take(o)
            out[...] = jnp.sum(ring_in[m].astype(F32), axis=0)

    weight_grad(0, img_t, img_back)
    fi[0:PI, :] = nt(img_back[0:PI, :], wi[...]).astype(BF)
    plane_send(0)

    grad = own_term[...]
    for o in range(1, N):
        grad = grad + term_in[term_x.take(o)].astype(F32)
    txt_back[...] = back_unit(grad, txt_unit[...], txt_inv[...]).astype(BF)
    weight_grad(1, txt_t, txt_back)
    ft[...] = nt(txt_back[...], wt[...]).astype(BF)
    save_txt = pltpu.make_async_copy(ft, ft_hbm, save_sem.at[1])
    save_txt.start()
    plane_send(1)
    for i in range(1, L):
        rows = slice(i * PI, (i + 1) * PI)
        fi[rows, :] = nt(img_back[rows, :], wi[...]).astype(BF)
    save_img = pltpu.make_async_copy(fi, fi_hbm, save_sem.at[0])
    save_img.start()
    ring_send(0)
    ring_send(1)
    full_send(0)
    full_send(1)
    result(0, gi_out)
    result(1, gt_out)

    save_img.wait()
    save_txt.wait()
    for copy in cores:
        copy.wait_send()
    for exchange in [text_x, term_x] + planes + rings + fulls:
        exchange.finish()


def shards(n_dp, n_neg, img_features, txt_features, w_img, w_txt, cap_len, pairs):
    L, PI, D = img_features.shape
    T = txt_features.shape[1]
    W = w_img.shape[1]
    N, H, r = n_neg, n_dp // 2, D // n_dp
    rows_i, rows_t = L * PI, L * T
    rr = r // N if r % (16 * N) == 0 else r
    vmem, dma = pltpu.VMEM, pltpu.SemaphoreType.DMA
    scratch = [
        vmem((rows_i, D), BF), vmem((rows_t, D), BF), vmem((D, W), BF), vmem((D, W), BF),
        vmem((D, rows_i), BF), vmem((D, rows_t), BF),
        vmem((rows_i, W), F32), vmem((rows_i, 1), F32), vmem((rows_i, W), BF),
        vmem((rows_t, W), F32), vmem((rows_t, 1), F32),
        vmem((N, rows_t, W), BF), vmem((N, rows_t, rows_i), F32), vmem((N, 8, rows_i), F32),
        vmem((N, N, 8, 128), F32), vmem((N, rows_t, rows_i), BF),
        vmem((N, rows_t, W), BF), vmem((rows_t, W), F32), vmem((N, rows_t, W), BF),
        vmem((rows_i, W), BF), vmem((rows_t, W), BF),
        vmem((2, 2, H, r, W), F32), vmem((2, H, r, W), BF), vmem((2, H, r, W), BF),
        vmem((2, H, r, W), BF), vmem((2, r, W), F32), vmem((2, H, r, W), BF),
        vmem((2, N, rr, W), F32), vmem((2, N, rr, W), BF),
        vmem((2, N, rr, W), BF), vmem((2, N, rr, W), BF),
        vmem((rows_i, D), BF), vmem((rows_t, D), BF),
        dma((4,)), dma((2,)),
        dma((N,)), dma((N,)), dma((N,)), dma((N,)), dma((N,)), dma((N,)),
        dma((2,)), dma((2,)), dma((2, H)), dma((2, H)),
        dma((2, N)), dma((2, N)), dma((2, N)), dma((2, N)),
    ]
    feat_img, feat_txt, final_img, final_txt = pl.pallas_call(
        functools.partial(kernel, (L, PI, T, D, W, N, n_dp)),
        out_shape=(
            jax.ShapeDtypeStruct((rows_i, D), BF),
            jax.ShapeDtypeStruct((rows_t, D), BF),
            jax.ShapeDtypeStruct((r, W), F32),
            jax.ShapeDtypeStruct((r, W), F32),
        ),
        in_specs=[pl.BlockSpec(memory_space=pl.ANY)] * 4
        + [pl.BlockSpec(memory_space=pltpu.SMEM)] * 2,
        out_specs=(pl.BlockSpec(memory_space=pl.ANY),) * 2
        + (pl.BlockSpec(memory_space=pltpu.VMEM),) * 2,
        scratch_shapes=scratch,
        compiler_params=pltpu.CompilerParams(
            collective_id=0, has_side_effects=True, vmem_limit_bytes=48 * 1024 * 1024
        ),
    )(
        img_features.reshape(rows_i, D),
        txt_features.reshape(rows_t, D),
        w_img,
        w_txt,
        cap_len,
        pairs,
    )
    return (
        feat_img.reshape(img_features.shape),
        feat_txt.reshape(txt_features.shape),
        final_img,
        final_txt,
    )


def solution(mesh):
    in_specs = (
        P(("dp", "neg"), None, None),
        P(("dp", "neg"), None, None),
        P(),
        P(),
        P(("dp", "neg")),
        P("dp", None),
    )
    out_specs = (
        P(("dp", "neg"), None, None),
        P(("dp", "neg"), None, None),
        P("dp", None),
        P("dp", None),
    )
    body = functools.partial(shards, mesh.shape["dp"], mesh.shape["neg"])
    return jax.shard_map(body, mesh=mesh, in_specs=in_specs, out_specs=out_specs, check_vma=False)
```

time: 199 us -> 47.5 us (0.24)
  waiting for transfers between devices: 127 us -> 0 us
  Pallas kernels: 0 us -> 38.6 us
  blocking collectives: 34.3 us -> 0 us
  between operations: 15.3 us -> 0.66 us
  matrix products: 9.68 us -> 0 us
  other arithmetic: 4.22 us -> 0 us
    reduce_scatter x3 -> x0, waiting for transfers between devices: 91.7 us -> none  [the longest x1 39.2 us: shards(): lax.psum_scatter(summed_txt, 'dp', scatter_dimension=0, tiled=True)]
    pallas_call x0 -> x1, Pallas kernels: none -> 38.6 us  [shards(): pl.pallas_call(functools.partial(kernel, (L, PI, T, D, W, N, n_dp)), out_...]
    psum x1 -> x0, waiting for transfers between devices: 35.3 us -> none  [shards(): summed_img, summed_txt = lax.psum((wgrad_img, wgrad_txt), 'neg')]
    unnamed x2 -> x0, blocking collectives: 20.5 us -> none
    all_gather x1 -> x0, blocking collectives: 13.8 us -> none  [shards(): lax.all_gather(txt_half.reshape(local_count, text_len, width), 'neg', axi...]
    dot_general x9 -> x0, matrix products: 9.68 us -> none  [the longest x1 1.87 us: shards(): jnp.dot(score_grad.T, img_half, preferred_element_type=jnp.float32)]
    convert_element_type x4 -> x0, other arithmetic: 2.2 us -> none  [the longest x1 1.01 us: shards(): txt_back = back_unit(txt_grad, txt_unit, txt_inv).astype(jnp.bfloat16)]
    unnamed x31 -> x16, local copies, waits for them, and re-layouts: 6.85 us -> 7.9 us
  transfers between devices with their start and end apart: 4 -> 0, of which waited for: 4 -> 0; matrix products, arithmetic and copies ran while one was open for 4% -> 0% of each run, Pallas kernels for 0% -> 0%
where the time goes in v1:
time: 47.5 us; the launch traced here: 47.2 us
  Pallas kernels  38.6 us (81%)
  local copies, waits for them, and re-layouts  7.9 us (17%)
  between operations  0.66 us (1%)
    pallas_call x1, Pallas kernels, shards(): pl.pallas_call(functools.partial(kernel, (L, PI, T, D, W, N, n_dp)), out_...  38.6 us
    unnamed x16, local copies, waits for them, and re-layouts  7.9 us

profile of v1, /device:TPU:0, one launch (start us, length us, event | category | flops | bytes accessed | tf_op | source)
XLA Modules:
  0.0 47.2 jit_solution(17997869176508565107)
XLA Ops:
  0.6 0.0 copy-start.4
  0.6 0.0 copy-start.5
  0.7 0.6 %copy-done.4 = s32[2]{0:T(128)S(1)} copy-done((s32[2]{0:T(128)S(1)}, s32[2]{0:T(128)}, u32[]{:S(2)}) %copy-start.4) | copy-done | bytes 32
  1.3 0.0 copy-done.5
  1.3 0.0 copy-start
  1.3 1.2 %copy-done = bf16[2,256,1024]{2,1,0:T(8,128)(2,1)S(1)} copy-done((bf16[2,256,1024]{2,1,0:T(8,128)(2,1)S(1)}, bf16[2,256,1024]{2,1,0:T(8,128)(2,1)}, u32[]{:S(2)}) %copy-start) | copy-done | bytes 1048600
  2.5 0.0 copy-start.1
  2.5 1.0 %copy-done.1 = bf16[1024,256]{1,0:T(8,128)(2,1)S(1)} copy-done((bf16[1024,256]{1,0:T(8,128)(2,1)S(1)}, bf16[1024,256]{1,0:T(8,128)(2,1)}, u32[]{:S(2)}) %copy-start.1) | copy-done | bytes 524312
  3.6 0.0 copy-start.2
  3.6 1.0 %copy-done.2 = bf16[1024,256]{1,0:T(8,128)(2,1)S(1)} copy-done((bf16[1024,256]{1,0:T(8,128)(2,1)S(1)}, bf16[1024,256]{1,0:T(8,128)(2,1)}, u32[]{:S(2)}) %copy-start.2) | copy-done | bytes 524312
  4.6 0.0 copy-start.3
  4.6 0.9 %copy-done.3 = bf16[2,64,1024]{2,1,0:T(8,128)(2,1)S(1)} copy-done((bf16[2,64,1024]{2,1,0:T(8,128)(2,1)S(1)}, bf16[2,64,1024]{2,1,0:T(8,128)(2,1)}, u32[]{:S(2)}) %copy-start.3) | copy-done | bytes 262168
  5.6 38.6 %shard_map.93 = (bf16[512,1024]{1,0:T(8,128)(2,1)S(1)}, bf16[128,1024]{1,0:T(8,128)(2,1)S(1)}, f32[128,256]{1,0:T(8,128)S(1)}, f32[128,256]{1,0:T(8,128)S(1)}) custom-call(bf16[512,1024]{1,0:T(8,128)(2,1)S(1)} %bitcast.4, bf16[128,1024]{1,0:T(8,128)(2,1)S(1)} %bitcast.6, bf16[1024,256]{1,0:T(8,128)(2,1)S(1)} %copy-done.1, bf16[1024,256]{1,0:T(8,128)(2,1)S(1)} %copy-done.2, ...), custom_call_target="tpu_custom_call" | custom-call | tf_op jit(solution)/shard_map/pallas_call | solution.py:365
  44.2 1.0 %copy.14 = bf16[2,256,1024]{2,1,0:T(8,128)(2,1)} copy(bf16[2,256,1024]{2,1,0:T(8,128)(2,1)S(1)} %bitcast.5) | data formatting | bytes 2097152
  45.2 0.7 %copy.15 = bf16[2,64,1024]{2,1,0:T(8,128)(2,1)} copy(bf16[2,64,1024]{2,1,0:T(8,128)(2,1)S(1)} %bitcast.7) | data formatting | bytes 524288
  45.9 0.7 %copy.16 = f32[128,256]{1,0:T(8,128)} copy(f32[128,256]{1,0:T(8,128)S(1)} %get-tuple-element.18) | data formatting | bytes 262144
  46.5 0.7 %copy.17 = f32[128,256]{1,0:T(8,128)} copy(f32[128,256]{1,0:T(8,128)S(1)} %get-tuple-element.19) | data formatting | bytes 262144
Async XLA Ops:
  0.6 0.7 %copy-start.4 = (s32[2]{0:T(128)S(1)}, s32[2]{0:T(128)}, u32[]{:S(2)}) copy-start(s32[2]{0:T(128)} %cap.1) | copy-start | bytes 28
  0.6 0.7 %copy-start.5 = (s32[1,8]{1,0:T(1,128)S(1)}, s32[1,8]{1,0:T(1,128)}, u32[]{:S(2)}) copy-start(s32[1,8]{1,0:T(1,128)} %pairs.1) | copy-start | bytes 100
  1.3 1.2 %copy-start = (bf16[2,256,1024]{2,1,0:T(8,128)(2,1)S(1)}, bf16[2,256,1024]{2,1,0:T(8,128)(2,1)}, u32[]{:S(2)}) copy-start(bf16[2,256,1024]{2,1,0:T(8,128)(2,1)} %param.6) | copy-start | bytes 3145732
  2.5 1.0 %copy-start.1 = (bf16[1024,256]{1,0:T(8,128)(2,1)S(1)}, bf16[1024,256]{1,0:T(8,128)(2,1)}, u32[]{:S(2)}) copy-start(bf16[1024,256]{1,0:T(8,128)(2,1)} %wi_hbm.1) | copy-start | bytes 1572868
  3.6 1.0 %copy-start.2 = (bf16[1024,256]{1,0:T(8,128)(2,1)S(1)}, bf16[1024,256]{1,0:T(8,128)(2,1)}, u32[]{:S(2)}) copy-start(bf16[1024,256]{1,0:T(8,128)(2,1)} %wt_hbm.1) | copy-start | bytes 1572868
  4.6 0.9 %copy-start.3 = (bf16[2,64,1024]{2,1,0:T(8,128)(2,1)S(1)}, bf16[2,64,1024]{2,1,0:T(8,128)(2,1)}, u32[]{:S(2)}) copy-start(bf16[2,64,1024]{2,1,0:T(8,128)(2,1)} %param.7) | copy-start | bytes 786436
